TPU v7x, 32 devices: a whole 2x2x4 slice. The times are simulated.
32 devices in a mesh: groups: 1, dev: 32 (over z, y, x, core).
Axes of the slice: x: 2, y: 2, z: 4, core: 2. Of those that a mesh axis runs over, the one named last changes fastest.
Arguments:
- hidden_in: bfloat16 [128, 4096], P(('groups', 'dev')), may hold values from -6 to 6
- queries: bfloat16 [128, 8192], P(('groups', 'dev')), may hold values from -160 to 160
- kv_cache: bfloat16 [128, 256, 1024], P(('groups', 'dev')), may hold values from -6 to 6
- new_kv: bfloat16 [128, 1024], P(('groups', 'dev')), may hold values from -6 to 6
- seq_lengths: int32 [128], P(('groups', 'dev')), may hold values from 2 to 256
- o_weight: bfloat16 [8192, 4096], P('dev'), may hold values from -0.59765625 to 0.59765625
- norm_gain: float32 [4096], replicated, may hold values from 0.5 to 1.5
- route_ids: int32 [128, 8], P(('groups', 'dev')), may hold values from 0 to 15, all different within a row; in each aligned block of 4 rows (0 to 3, 4 to 7, ...) at most 2 rows name the same one
- route_weights: float32 [128, 8], P(('groups', 'dev')), may hold values from 0.05 to 0.5
- w_gate_up: bfloat16 [32, 4096, 768], P('dev'), may hold values from -0.09375 to 0.09375
- w_down: bfloat16 [32, 384, 4096], P('dev'), may hold values from -0.21875 to 0.21875
Outputs:
- layer_out: bfloat16 [128, 4096], P(('groups', 'dev'))
Inputs may be any that keep to these rules, and one draw needn't show every extreme that they name: `route_ids`: a token names 8 different experts; in the rows of one device no expert is named by more than 2 tokens.
All inputs are finite; a program needn't handle non-finite values.
Results may differ from a plain program's by a relative error of at most 0.006.
Values may be sent and summed in bfloat16 or wider, within the bound.
A program may use at most 64 MiB of HBM per device.

v0:
```python
import jax
import jax.numpy as jnp
from jax import lax
from jax.sharding import PartitionSpec as P

HEADS = 64
KVH = 4
HD = 128
TOPK = 8
HSPLIT = 2


def attend(queries, kv_cache, new_kv, seq_lengths):
    seq_count = queries.shape[0]
    ctx_len = kv_cache.shape[1]
    per_group = HEADS // KVH
    kv_width = KVH * HD
    score_scale = HD ** (-0.5)
    query_heads = queries.reshape(seq_count, KVH, per_group, HD)
    cache_keys = kv_cache[:, :, :kv_width].reshape(seq_count, ctx_len, KVH, HD)
    cache_values = kv_cache[:, :, kv_width:].reshape(seq_count, ctx_len, KVH, HD)
    fresh_key = new_kv[:, :kv_width].reshape(seq_count, KVH, HD)
    fresh_value = new_kv[:, kv_width:].astype(jnp.float32).reshape(seq_count, KVH, HD)
    cache_scores = (
        jnp.einsum("bgqd,bjgd->bgqj", query_heads, cache_keys, preferred_element_type=jnp.float32)
        * score_scale
    )
    fresh_scores = (
        jnp.einsum("bgqd,bgd->bgq", query_heads, fresh_key, preferred_element_type=jnp.float32)
        * score_scale
    )
    live_mask = jnp.arange(ctx_len, dtype=jnp.int32)[None, :] < seq_lengths[:, None]
    cache_scores = jnp.where(live_mask[:, None, None, :], cache_scores, -jnp.inf)
    peak_score = jnp.maximum(jnp.max(cache_scores, axis=-1), fresh_scores)
    cache_exp = jnp.exp(cache_scores - peak_score[..., None])
    fresh_exp = jnp.exp(fresh_scores - peak_score)
    denominator = jnp.sum(cache_exp, axis=-1) + fresh_exp
    cache_probs = (cache_exp / denominator[..., None]).astype(jnp.bfloat16)
    fresh_probs = (fresh_exp / denominator).astype(jnp.bfloat16)
    attended = jnp.einsum(
        "bgqj,bjgd->bgqd", cache_probs, cache_values, preferred_element_type=jnp.float32
    )
    attended = attended + fresh_probs.astype(jnp.float32)[..., None] * fresh_value[:, :, None, :]
    return attended.astype(jnp.bfloat16).reshape(seq_count, HEADS * HD)


def rms_normed(resid, norm_gain):
    mean_square = jnp.mean(resid * resid, axis=-1, keepdims=True)
    return (resid * lax.rsqrt(mean_square + 1e-06) * norm_gain).astype(jnp.bfloat16)


def slot_pick(flat_ids, experts, capacity):
    matches = flat_ids == experts[:, None]
    slot_rank = jnp.cumsum(matches.astype(jnp.int32), axis=1) - 1
    slot_numbers = jnp.arange(capacity, dtype=jnp.int32)
    picked = matches[:, None, :] & (slot_rank[:, None, :] == slot_numbers[None, :, None])
    return picked.astype(jnp.float32)


def expert_rows(gathered_rows, gate_up, down):
    gate_up_out = jnp.einsum(
        "smx,xf->smf", gathered_rows, gate_up, preferred_element_type=jnp.float32
    )
    split_at = gate_up.shape[1] // 2
    activated = (jax.nn.silu(gate_up_out[..., :split_at]) * gate_up_out[..., split_at:]).astype(
        jnp.bfloat16
    )
    return jnp.einsum("smf,fx->smx", activated, down, preferred_element_type=jnp.float32).astype(
        jnp.bfloat16
    )


def send_back(expert_out):
    return lax.all_to_all(expert_out, "dev", split_axis=0, concat_axis=0, tiled=True)


def shards(
    hidden_in,
    queries,
    kv_cache,
    new_kv,
    seq_lengths,
    o_weight,
    norm_gain,
    route_ids,
    route_weights,
    w_gate_up,
    w_down,
):
    seq_count = hidden_in.shape[0]
    dev_count = lax.axis_size("dev")
    device_index = lax.axis_index("dev")
    capacity = max(2, seq_count * TOPK // (dev_count // HSPLIT))
    route_total = seq_count * TOPK
    attn = attend(queries, kv_cache, new_kv, seq_lengths)
    gathered = lax.all_to_all(attn, "dev", split_axis=1, concat_axis=0, tiled=True)
    dest_experts = jnp.arange(dev_count, dtype=jnp.int32) // HSPLIT
    own_flat = jnp.broadcast_to(route_ids.reshape(1, route_total), (dev_count, route_total))
    own_pick = slot_pick(own_flat, dest_experts, capacity)
    slot_coef = (
        (own_pick * route_weights.reshape(1, 1, route_total))
        .reshape(dev_count, capacity, seq_count, TOPK)
        .sum(axis=-1)
    )
    partial_value = jnp.dot(gathered, o_weight, preferred_element_type=jnp.float32)
    own_rows = lax.dynamic_slice_in_dim(
        partial_value, device_index * seq_count, seq_count, 0
    ) + hidden_in.astype(jnp.float32)
    partial_value = lax.dynamic_update_slice_in_dim(
        partial_value, own_rows, device_index * seq_count, 0
    )
    resid_all = lax.psum(partial_value, "dev")
    resid = lax.dynamic_slice_in_dim(resid_all, device_index * seq_count, seq_count, 0)
    normed_all = rms_normed(resid_all, norm_gain).reshape(dev_count, seq_count, resid_all.shape[1])
    every_route = lax.all_gather(route_ids, "dev", axis=0, tiled=True)
    source_flat = every_route.reshape(dev_count, route_total)
    my_expert = jnp.full((dev_count,), device_index // HSPLIT, jnp.int32)
    source_pick = slot_pick(source_flat, my_expert, capacity)
    source_tokens = source_pick.reshape(dev_count, capacity, seq_count, TOPK).sum(axis=-1)
    incoming = jnp.einsum(
        "smt,stx->smx",
        source_tokens.astype(jnp.bfloat16),
        normed_all,
        preferred_element_type=jnp.float32,
    ).astype(jnp.bfloat16)
    returned_rows = send_back(expert_rows(incoming, w_gate_up[0], w_down[0]))
    routed_sum = jnp.einsum(
        "dmt,dmx->tx", slot_coef, returned_rows.astype(jnp.float32), precision=lax.Precision.HIGHEST
    )
    return (resid + routed_sum).astype(jnp.bfloat16)


def solution(mesh):
    in_specs = (
        P(("groups", "dev"), None),
        P(("groups", "dev"), None),
        P(("groups", "dev"), None, None),
        P(("groups", "dev"), None),
        P(("groups", "dev")),
        P("dev", None),
        P(),
        P(("groups", "dev"), None),
        P(("groups", "dev"), None),
        P("dev", None, None),
        P("dev", None, None),
    )
    out_specs = P(("groups", "dev"), None)
    return jax.shard_map(shards, mesh=mesh, in_specs=in_specs, out_specs=out_specs, check_vma=False)
```

profile of v0, /device:TPU:0, one launch (start us, length us, event | category | flops | bytes accessed | tf_op | source)
XLA Modules:
  0.0 211.4 jit_solution(12920339566061923982)
XLA Ops:
  6.5 3.2 %fusion.20 = (bf16[4,256,512]{2,1,0:T(8,128)(2,1)}, bf16[4,256,512]{2,1,0:T(8,128)(2,1)}) fusion(bf16[4,256,1024]{2,1,0:T(8,128)(2,1)} %param.13), kind=kLoop, calls=%fused_computation.50 | loop fusion | bytes 4194304 | tf_op jit(solution)/shard_map/slice | solution.py:20
  9.7 2.3 %copy.55 = bf16[4,256,512]{1,2,0:T(8,128)(2,1)} copy(bf16[4,256,512]{2,1,0:T(8,128)(2,1)} %get-tuple-element.7) | data formatting | bytes 2097152
  12.3 1.6 fusion.21
  13.9 0.2 fusion.9
  14.1 2.3 %copy.56 = bf16[4,256,512]{1,2,0:T(8,128)(2,1)} copy(bf16[4,256,512]{2,1,0:T(8,128)(2,1)} %get-tuple-element.8) | data formatting | bytes 2097152
  16.4 1.6 fusion.6
  18.1 0.7 copy.42
  18.8 7.3 %all-to-all-start = ((bf16[4,32,256]{2,0,1:T(4,128)(2,1)}), bf16[4,32,256]{2,0,1:T(4,128)(2,1)S(1)}, u32[]{:S(2)}, u32[]{:S(2)}) async-start(bf16[4,32,256]{2,0,1:T(4,128)(2,1)} %copy.42), calls=%async_computation | async-start | bytes 131072 | tf_op jit(solution)/shard_map/all_to_all | solution.py:96
  26.2 7.4 %all-to-all-done = bf16[4,32,256]{2,0,1:T(4,128)(2,1)S(1)} async-done(((bf16[4,32,256]{2,0,1:T(4,128)(2,1)}), bf16[4,32,256]{2,0,1:T(4,128)(2,1)S(1)}, u32[]{:S(2)}, u32[]{:S(2)}) %all-to-all-start) | async-done | bytes 65568 | tf_op jit(solution)/shard_map/all_to_all | solution.py:96
  33.6 3.3 %fusion.23 = f32[128,4096]{1,0:T(8,128)} fusion(bf16[128,256]{1,0:T(8,128)(2,1)S(1)} %all_to_all.20, bf16[256,4096]{1,0:T(8,128)(2,1)} %param.16), kind=kOutput, calls=%fused_computation.53 | convolution fusion | flops 268435456 | bytes 4259840 | tf_op jit(solution)/shard_map/dot_general | solution.py:105
  36.9 1.6 add_dynamic-update-slice_fusion
  38.5 37.8 %all-gather = s32[32,4,8]{2,1,0:T(4,128)S(1)} all-gather(s32[1,4,8]{2,1,0:T(4,128)S(1)} %bitcast.49), channel_id=1, replica_groups=mesh['groups'=1,'dev'=32] {'dev'}, dimensions={0}, use_global_device_ids=true | all-gather | bytes 4224 | tf_op jit(solution)/shard_map/all_gather | solution.py:115
  76.9 92.3 %all-reduce.2.cloned.1.call-done = f32[128,4096]{1,0:T(8,128)} async-done(((f32[128,4096]{1,0:T(8,128)}), f32[128,4096]{1,0:T(8,128)}) %all-reduce.2.cloned.1.call-update) | async-done | bytes 2097168 | tf_op jit(solution)/shard_map/psum | solution.py:112
  169.3 2.0 multiply_reduce_fusion
  171.2 0.2 copy-done.1
  171.5 1.3 multiply_convert_fusion
  172.7 2.3 %reshape.180 = bf16[32,4,4096]{2,1,0:T(4,128)(2,1)} reshape(bf16[128,4096]{1,0:T(8,128)(2,1)} %multiply_convert_fusion) | data formatting | bytes 2097152 | tf_op jit(solution)/shard_map/reshape | solution.py:114
  175.0 1.9 convolution_convert_fusion.1
  176.9 4.2 %fusion = f32[32,2,768]{2,0,1:T(8,128)S(1)} fusion(bf16[1,4096,768]{2,1,0:T(8,128)(2,1)} %param.20, bf16[32,2,4096]{2,1,0:T(2,128)(2,1)S(1)} %convolution_convert_fusion.1), kind=kOutput, calls=%fused_computation | convolution fusion | flops 402653184 | bytes 7012352 | tf_op jit(solution)/shard_map/smx,xf->smf/dot_general | solution.py:61
  181.1 0.7 convolution_convert_fusion
  181.8 1.4 copy.49
  183.2 3.6 %all-to-all-start.1 = ((bf16[32,2,4096]{2,1,0:T(2,128)(2,1)}), bf16[32,2,4096]{2,1,0:T(2,128)(2,1)}, u32[]{:S(2)}, u32[]{:S(2)}) async-start(bf16[32,2,4096]{2,1,0:T(2,128)(2,1)} %copy.49), calls=%async_computation.1 | async-start | bytes 1048576 | tf_op jit(solution)/shard_map/all_to_all | solution.py:74
  187.4 14.9 %all-to-all-done.1 = bf16[32,2,4096]{2,1,0:T(2,128)(2,1)} async-done(((bf16[32,2,4096]{2,1,0:T(2,128)(2,1)}), bf16[32,2,4096]{2,1,0:T(2,128)(2,1)}, u32[]{:S(2)}, u32[]{:S(2)}) %all-to-all-start.1) | async-done | bytes 524320 | tf_op jit(solution)/shard_map/all_to_all | solution.py:74
  202.4 2.2 %fusion.3 = bf16[4,4096]{1,0:T(4,128)(2,1)} fusion(f32[32,2,4]{0,2,1:T(4,128)S(1)} %select_reduce_fusion, bf16[32,2,4096]{2,1,0:T(2,128)(2,1)} %all-to-all-done.1, f32[128,4096]{1,0:T(8,128)} %all-reduce.2.cloned.1.call-done, s32[]{:T(128)S(6)} %select_n.26), kind=kOutput, calls=%fused_computation.6 | convolution fusion | flops 12615680 | bytes 623620 | tf_op jit(solution)/shard_map/dmt,dmx->tx/dot_general | solution.py:127
  (46 shorter events, 1.6 us)
Async XLA Ops:
  6.5 174.6 %copy-start = (bf16[1,384,4096]{2,1,0:T(8,128)(2,1)S(1)}, bf16[1,384,4096]{2,1,0:T(8,128)(2,1)}, u32[]{:S(2)}) copy-start(bf16[1,384,4096]{2,1,0:T(8,128)(2,1)} %param.21) | copy-start | bytes 9437188
  9.7 2.3 %copy-start.2 = (bf16[4,8192]{1,0:T(4,128)(2,1)S(1)}, bf16[4,8192]{1,0:T(4,128)(2,1)}, u32[]{:S(2)}) copy-start(bf16[4,8192]{1,0:T(4,128)(2,1)} %param.12) | copy-start | bytes 196612
  9.7 2.3 %copy-start.8 = (s32[4]{0:T(128)S(1)}, s32[4]{0:T(128)}, u32[]{:S(2)}) copy-start(s32[4]{0:T(128)} %param.15) | copy-start | bytes 52
  9.7 2.4 %copy-start.6 = (bf16[4,1024]{1,0:T(4,128)(2,1)S(1)}, bf16[4,1024]{1,0:T(4,128)(2,1)}, u32[]{:S(2)}) copy-start(bf16[4,1024]{1,0:T(4,128)(2,1)} %param.14) | copy-start | bytes 24580
  18.8 14.7 %all-to-all-start = ((bf16[4,32,256]{2,0,1:T(4,128)(2,1)}), bf16[4,32,256]{2,0,1:T(4,128)(2,1)S(1)}, u32[]{:S(2)}, u32[]{:S(2)}) async-start(bf16[4,32,256]{2,0,1:T(4,128)(2,1)} %copy.42), calls=%async_computation | async-start | bytes 131072 | tf_op jit(solution)/shard_map/all_to_all | solution.py:96
  26.1 143.1 %all-reduce.2.cloned.1.call-start = ((), (), s32[]{:S(2)}) async-start(), calls=%async_computation.2 | async-start | bytes 4194304 | tf_op jit(solution)/shard_map/psum | solution.py:112
  33.6 3.4 %copy-start.3 = (bf16[4,4096]{1,0:T(4,128)(2,1)S(1)}, bf16[4,4096]{1,0:T(4,128)(2,1)}, u32[]{:S(2)}) copy-start(bf16[4,4096]{1,0:T(4,128)(2,1)} %param.11) | copy-start | bytes 98308
  36.9 1.6 copy-start.4
  38.5 132.8 %copy-start.5 = (f32[4096]{0:T(1024)S(1)}, f32[4096]{0:T(1024)}, u32[]{:S(2)}) copy-start(f32[4096]{0:T(1024)} %param.17) | copy-start | bytes 49156
  169.3 2.2 %copy-start.1 = (f32[128,4096]{1,0:T(8,128)S(1)}, f32[128,4096]{1,0:T(8,128)}, u32[]{:S(2)}) copy-start(f32[128,4096]{1,0:T(8,128)} %all-reduce.2.cloned.1.call-done) | copy-start | bytes 6291460
  181.8 5.5 %copy-start.7 = (f32[4,8]{1,0:T(4,128)S(1)}, f32[4,8]{1,0:T(4,128)}, u32[]{:S(2)}) copy-start(f32[4,8]{1,0:T(4,128)} %param.19) | copy-start | bytes 388
  183.2 19.2 %all-to-all-start.1 = ((bf16[32,2,4096]{2,1,0:T(2,128)(2,1)}), bf16[32,2,4096]{2,1,0:T(2,128)(2,1)}, u32[]{:S(2)}, u32[]{:S(2)}) async-start(bf16[32,2,4096]{2,1,0:T(2,128)(2,1)} %copy.49), calls=%async_computation.1 | async-start | bytes 1048576 | tf_op jit(solution)/shard_map/all_to_all | solution.py:74
Sparse Core Ops, SparseCore 0:
  38.6 130.5 all-reduce.1
where the time goes:
time: 212 us; the launch traced here: 211 us
  waiting for transfers between devices  115 us (54%)
  blocking collectives  37.8 us (18%)
  matrix products  15.7 us (7%)
  between operations  13.5 us (6%)
  local copies, waits for them, and re-layouts  12.9 us (6%)
  starting transfers between devices  11 us (5%)
  other arithmetic  5.83 us (3%)
    psum x1, waiting for transfers between devices, shards(): resid_all = lax.psum(partial_value, 'dev')  92.3 us
    all_gather x1, blocking collectives, shards(): every_route = lax.all_gather(route_ids, 'dev', axis=0, tiled=True)  37.8 us
    all_to_all x1, waiting for transfers between devices, send_back(): lax.all_to_all(expert_out, 'dev', split_axis=0, concat_axis=0, tiled=True)  14.9 us
    all_to_all x1, waiting for transfers between devices, shards(): lax.all_to_all(attn, 'dev', split_axis=1, concat_axis=0, tiled=True)  7.36 us
    all_to_all x1, starting transfers between devices, shards(): lax.all_to_all(attn, 'dev', split_axis=1, concat_axis=0, tiled=True)  7.3 us
    unnamed x21, local copies, waits for them, and re-layouts  4.88 us
  transfers between devices with their start and end apart: 3, of which 3 were waited for; matrix products, arithmetic and copies ran while one was open for 1% of the time, Pallas kernels for 0%

commit v1 on v0

v1 whole, which is shorter than its diff:
```python
import functools

import jax
import jax.numpy as jnp
from jax import lax
from jax.experimental import pallas as pl
from jax.experimental.pallas import tpu as pltpu
from jax.sharding import PartitionSpec as P

HEADS = 64
KVH = 4
HD = 128
TOPK = 8
PLANE = 8
CHUNKS = 4
SUB = 4
F32 = jnp.float32
BF16 = jnp.bfloat16


def dev_copy(src, dst, send, recv, target):
    return pltpu.make_async_remote_copy(
        src_ref=src, dst_ref=dst, send_sem=send, recv_sem=recv,
        device_id={"dev": target}, device_id_type=pl.DeviceIdType.MESH,
    )


def pick_matrix(tokens, cols, block, offset, z_count):
    row = lax.broadcasted_iota(jnp.int32, (tokens, cols), 0)
    col = lax.broadcasted_iota(jnp.int32, (tokens, cols), 1)
    zr = z_count * 4
    b = row & 3
    z = (row >> 2) & (z_count - 1)
    rest = row // zr
    xy = rest & 3
    core = rest >> 2
    src = z * 8 + xy * 2 + core
    return jnp.where(col == src * block + offset + b, 1.0, 0.0).astype(BF16)


def kernel(
    n, lens, hid, q_ref, kv_hbm, new_ref, gain_ref, ids_ref, rw_ref, wo_hbm, wgu_hbm, wd_hbm,
    out_ref,
    kv, wo, wgu, wd, load_sem,
    asend, arecv, a_ss, a_rs, csend, crecv, c_ss, c_rs,
    yb, yf, crx, qf, qb, prx, zb, zf, zrx, res,
    core_ss, core_rs, pl_ss, pl_rs, z_ss, z_rs,
    nz, gx, nz_ss, nz_rs, np_ss, np_rs, nc_ss, nc_rs,
    gu, act, coef,
):
    me = lax.axis_index("dev")
    zc = n // PLANE
    zr = zc * 4
    tokens = 4 * n
    half = tokens // 2
    my_z = me // PLANE
    my_p = me % PLANE
    my_xy = my_p // 2
    my_core = my_p % 2
    mate = my_z * PLANE + my_xy * 2 + (1 - my_core)
    d_model = out_ref.shape[1]
    cw = d_model // CHUNKS
    sw = cw // SUB
    ctx = kv.shape[1]
    kvw = KVH * HD
    per_group = HEADS // KVH
    hpd = HEADS // n
    dpg = n // KVH
    block = asend.shape[1]

    def xy_peer(j):
        return my_z * PLANE + ((my_xy + j) % 4) * 2 + my_core

    def z_peer(j):
        return ((my_z + j) % zc) * PLANE + my_p

    barrier = pltpu.get_barrier_semaphore()

    loads = [
        pltpu.make_async_copy(kv_hbm, kv, load_sem.at[0]),
        pltpu.make_async_copy(wo_hbm, wo, load_sem.at[1]),
        pltpu.make_async_copy(wgu_hbm.at[0], wgu, load_sem.at[2]),
        pltpu.make_async_copy(wd_hbm.at[0], wd, load_sem.at[3]),
    ]
    loads[0].start()

    @pl.loop(1, n)
    def _(k):
        pl.semaphore_signal(
            barrier, inc=1, device_id={"dev": (me + k) % n}, device_id_type=pl.DeviceIdType.MESH
        )

    for load in loads[1:]:
        load.start()

    lane = lax.broadcasted_iota(jnp.int32, (4, 128), 1)
    ids = ids_ref[...]
    rw = rw_ref[...]
    own_coef = jnp.zeros((4, 128), F32)
    for k in range(TOPK):
        own_coef = own_coef + jnp.where(ids[:, k:k + 1] == (lane & 63), rw[:, k:k + 1], 0.0)
    high = own_coef.astype(BF16).astype(F32)
    packed = jnp.where(lane < 64, high, own_coef - high)
    csend[...] = jnp.concatenate([packed] * 4, axis=0).astype(BF16)

    rows = per_group * 4
    row_b = lax.broadcasted_iota(jnp.int32, (rows, 1), 0) & 3
    length = jnp.full((rows, 1), lens[0], jnp.int32)
    for b in range(1, 4):
        length = jnp.where(row_b == b, lens[b], length)
    live = lax.broadcasted_iota(jnp.int32, (rows, ctx), 1) < length
    new = new_ref[...].astype(F32)
    loads[0].wait()
    for g in range(KVH):
        q_all = q_ref[:, g * per_group * HD:(g + 1) * per_group * HD].astype(F32)
        qg = jnp.concatenate([q_all[:, r * HD:(r + 1) * HD] for r in range(per_group)], axis=0)
        k_own = jnp.concatenate([new[:, g * HD:(g + 1) * HD]] * per_group, axis=0)
        v_own = jnp.concatenate([new[:, kvw + g * HD:kvw + (g + 1) * HD]] * per_group, axis=0)
        q16 = qg.astype(BF16)
        scores = None
        for b in range(4):
            s_b = lax.dot_general(
                q16, kv[b, :, g * HD:(g + 1) * HD], (((1,), (1,)), ((), ())),
                preferred_element_type=F32,
            )
            scores = s_b if b == 0 else jnp.where(row_b == b, s_b, scores)
        scale = HD ** (-0.5)
        scores = jnp.where(live, scores * scale, -jnp.inf)
        fresh = jnp.sum(qg * k_own, axis=1, keepdims=True) * scale
        peak = jnp.maximum(jnp.max(scores, axis=1, keepdims=True), fresh)
        e = jnp.exp(scores - peak)
        e_own = jnp.exp(fresh - peak)
        den = jnp.sum(e, axis=1, keepdims=True) + e_own
        probs = e / den
        p_own = (e_own / den).astype(BF16).astype(F32)
        acc = p_own * v_own
        for b in range(4):
            p_b = jnp.where(row_b == b, probs, 0.0).astype(BF16)
            acc = acc + jnp.dot(
                p_b, kv[b, :, kvw + g * HD:kvw + (g + 1) * HD], preferred_element_type=F32
            )
        acc = acc.astype(BF16).astype(F32)
        for i in range(dpg):
            piece = acc[i * hpd * 4:(i + 1) * hpd * 4, :]
            if piece.shape[0] < block:
                piece = jnp.concatenate([piece] * (block // piece.shape[0]), axis=0)
            asend[g * dpg + i] = piece

        if g == 0:
            pl.semaphore_wait(barrier, n - 1)

            @pl.loop(1, n)
            def _(k):
                target = (me + k) % n
                dev_copy(csend, crecv.at[me], c_ss.at[target], c_rs.at[me], target).start()

        @pl.loop(0, dpg)
        def _(i):
            target = g * dpg + (me + i) % dpg

            @pl.when(target != me)
            def _():
                dev_copy(
                    asend.at[target], arecv.at[me], a_ss.at[target], a_rs.at[me], target
                ).start()

    arecv[me] = asend[me]
    crecv[me] = csend[...]

    @pl.loop(1, n)
    def _(k):
        source = (me + k) % n
        dev_copy(
            asend.at[source], arecv.at[source], a_ss.at[source], a_rs.at[source], source
        ).wait()

    x_all = arecv[...].reshape(n * block, HD).astype(BF16)
    gathered = jnp.concatenate(
        [
            jnp.dot(
                pick_matrix(tokens, n * block, block, rr * 4, zc), x_all,
                preferred_element_type=F32,
            )
            for rr in range(hpd)
        ],
        axis=1,
    ).astype(BF16)

    def reduce_chunks(t, make, done):
        cores = [
            dev_copy(yb.at[t, k, 1 - my_core], crx.at[t, k], core_ss.at[t, k], core_rs.at[t, k], mate)
            for k in range(CHUNKS)
        ]
        planes = [
            [
                dev_copy(
                    qb.at[t, k, (my_xy + j) % 4], prx.at[t, k, j - 1],
                    pl_ss.at[t, k, j - 1], pl_rs.at[t, k, j - 1], xy_peer(j),
                )
                for j in range(1, 4)
            ]
            for k in range(CHUNKS)
        ]
        lines = [
            [
                dev_copy(
                    zb.at[t, k, (my_z + j) % zc], zrx.at[t, k, j - 1],
                    z_ss.at[t, k, j - 1], z_rs.at[t, k, j - 1], z_peer(j),
                )
                for j in range(1, zc)
            ]
            for k in range(CHUNKS)
        ]
        for k in range(CHUNKS):
            y = make(k).reshape(2, 4, zr, cw)
            yb[t, k] = y.astype(BF16)
            cores[k].start()
            yf[k] = y
        for k in range(CHUNKS):
            cores[k].wait_recv()
            total = yf[k, my_core] + crx[t, k].astype(F32)
            qb[t, k] = total.astype(BF16)
            for copy in planes[k]:
                copy.start()
            qf[k] = total
        for k in range(CHUNKS):
            total = qf[k, my_xy]
            for j in range(1, 4):
                planes[k][j - 1].wait_recv()
                total = total + prx[t, k, j - 1].astype(F32)
            for z in range(zc):
                part = jnp.concatenate(
                    [total[4 * z:4 * z + 4, s * sw:(s + 1) * sw] for s in range(SUB)], axis=0
                )
                zb[t, k, z] = part.astype(BF16)
                zf[k, z] = part
            for copy in lines[k]:
                copy.start()
        for k in range(CHUNKS):
            total = zf[k, my_z]
            for j in range(1, zc):
                lines[k][j - 1].wait_recv()
                total = total + zrx[t, k, j - 1].astype(F32)
            done(k, total)
        for k in range(CHUNKS):
            cores[k].wait_send()
            for copy in planes[k] + lines[k]:
                copy.wait_send()

    loads[1].wait()

    def project(k):
        return jnp.dot(gathered, wo[:, k * cw:(k + 1) * cw], preferred_element_type=F32)

    hidden = hid[...].astype(F32)
    squares = []

    def add_hidden(k, total):
        own = jnp.concatenate(
            [hidden[:, k * cw + s * sw:k * cw + (s + 1) * sw] for s in range(SUB)], axis=0
        )
        value = total + own
        res[k] = value
        squares.append(jnp.sum(value * value, axis=1, keepdims=True))

    reduce_chunks(0, project, add_hidden)

    square = sum(squares[1:], squares[0])
    square = square[0:4] + square[4:8] + square[8:12] + square[12:16]
    inverse = lax.rsqrt(square / d_model + 1e-06)
    inverse = jnp.concatenate([inverse] * SUB, axis=0)

    line_out = []
    for k in range(CHUNKS):
        gain = jnp.concatenate(
            [
                jnp.broadcast_to(
                    gain_ref[:, k * cw + s * sw:k * cw + (s + 1) * sw], (4, sw)
                )
                for s in range(SUB)
            ],
            axis=0,
        )
        nz[k, my_z] = (res[k] * inverse * gain).astype(BF16)
        for j in range(1, zc):
            copy = dev_copy(
                nz.at[k, my_z], nz.at[k, my_z], nz_ss.at[k, j - 1], nz_rs.at[k, j - 1], z_peer(j)
            )
            copy.start()
            line_out.append(copy)
    plane_out = []
    for k in range(CHUNKS):
        for j in range(1, zc):
            from_z = (my_z + zc - j) % zc
            dev_copy(
                nz.at[k, from_z], nz.at[k, from_z], nz_ss.at[k, j - 1], nz_rs.at[k, j - 1], z_peer(j)
            ).wait_recv()
        parts = []
        for z in range(zc):
            value = nz[k, z].astype(F32)
            parts.append(
                jnp.concatenate([value[4 * s:4 * s + 4, :] for s in range(SUB)], axis=1)
            )
        gx[k, my_core, my_xy] = jnp.concatenate(parts, axis=0).astype(BF16)
        for j in range(1, 4):
            mine = gx.at[k, my_core, my_xy]
            copy = dev_copy(mine, mine, np_ss.at[k, j - 1], np_rs.at[k, j - 1], xy_peer(j))
            copy.start()
            plane_out.append(copy)
    core_out = []
    for k in range(CHUNKS):
        for j in range(1, 4):
            theirs = gx.at[k, my_core, (my_xy + 4 - j) % 4]
            dev_copy(theirs, theirs, np_ss.at[k, j - 1], np_rs.at[k, j - 1], xy_peer(j)).wait_recv()
        copy = dev_copy(gx.at[k, my_core], gx.at[k, my_core], nc_ss.at[k], nc_rs.at[k], mate)
        copy.start()
        core_out.append(copy)

    @pl.loop(1, n)
    def _(k):
        source = (me + k) % n
        dev_copy(csend, crecv.at[source], c_ss.at[source], c_rs.at[source], source).wait()

    spread = jnp.dot(
        pick_matrix(tokens, n * 16, 16, 0, zc), crecv[...].reshape(n * 16, 128),
        preferred_element_type=F32,
    )
    lane_t = lax.broadcasted_iota(jnp.int32, (tokens, 128), 1) & 63
    coef[...] = jnp.broadcast_to(
        jnp.sum(jnp.where(lane_t == me // 2, spread, 0.0), axis=1, keepdims=True), (tokens, 128)
    )

    loads[2].wait()
    for k in range(CHUNKS):
        mates = gx.at[k, 1 - my_core]
        dev_copy(mates, mates, nc_ss.at[k], nc_rs.at[k], mate).wait_recv()
        part = jnp.dot(
            gx[k].reshape(tokens, cw), wgu[k * cw:(k + 1) * cw, :], preferred_element_type=F32
        )
        if k == 0:
            gu[...] = part
        else:
            gu[...] += part
    for copy in line_out + plane_out + core_out:
        copy.wait_send()
    ff = gu.shape[1] // 2
    gate = gu[:, :ff]
    act[...] = (gate / (1.0 + jnp.exp(-gate)) * gu[:, ff:]).astype(BF16)

    loads[3].wait()

    def expert_out(k):
        y = jnp.dot(act[...], wd[:, k * cw:(k + 1) * cw], preferred_element_type=F32)
        return y.astype(BF16).astype(F32) * coef[:, 0:1]

    def finish(k, total):
        value = (res[k] + total).astype(out_ref.dtype).astype(F32)
        for s in range(SUB):
            lo = k * cw + s * sw
            out_ref[:, lo:lo + sw] = value[4 * s:4 * s + 4, :].astype(out_ref.dtype)

    reduce_chunks(1, expert_out, finish)


def solution(mesh):
    n = mesh.shape["dev"]

    def step(hidden, queries, kv_cache, new_kv, lens, wo, gain, ids, rw, wgu, wd):
        seqs, d_model = hidden.shape
        zc = n // PLANE
        zr = zc * 4
        tokens = n * seqs
        cw = d_model // CHUNKS
        sw = cw // SUB
        block = max(8, HEADS // n * 4)
        dma = pltpu.SemaphoreType.DMA
        vmem = pltpu.VMEM
        any_spec = pl.BlockSpec(memory_space=pl.ANY)
        v_spec = pl.BlockSpec(memory_space=pltpu.VMEM)
        zp = max(1, zc - 1)
        return pl.pallas_call(
            functools.partial(kernel, n),
            out_shape=jax.ShapeDtypeStruct((seqs, d_model), BF16),
            in_specs=[
                pl.BlockSpec(memory_space=pltpu.SMEM), v_spec, v_spec, any_spec, v_spec, v_spec,
                v_spec, v_spec, any_spec, any_spec, any_spec,
            ],
            out_specs=v_spec,
            scratch_shapes=[
                vmem(kv_cache.shape, BF16), vmem(wo.shape, BF16), vmem(wgu.shape[1:], BF16),
                vmem(wd.shape[1:], BF16), dma((4,)),
                vmem((n, block, HD), F32), vmem((n, block, HD), F32), dma((n,)), dma((n,)),
                vmem((16, 128), BF16), vmem((n, 16, 128), BF16), dma((n,)), dma((n,)),
                vmem((2, CHUNKS, 2, 4, zr, cw), BF16), vmem((CHUNKS, 2, 4, zr, cw), F32),
                vmem((2, CHUNKS, 4, zr, cw), BF16), vmem((CHUNKS, 4, zr, cw), F32),
                vmem((2, CHUNKS, 4, zr, cw), BF16), vmem((2, CHUNKS, 3, zr, cw), BF16),
                vmem((2, CHUNKS, zc, 4 * SUB, sw), BF16), vmem((CHUNKS, zc, 4 * SUB, sw), F32),
                vmem((2, CHUNKS, zp, 4 * SUB, sw), BF16), vmem((CHUNKS, 4 * SUB, sw), F32),
                dma((2, CHUNKS)), dma((2, CHUNKS)), dma((2, CHUNKS, 3)), dma((2, CHUNKS, 3)),
                dma((2, CHUNKS, zp)), dma((2, CHUNKS, zp)),
                vmem((CHUNKS, zc, 4 * SUB, sw), BF16), vmem((CHUNKS, 2, 4, zr, cw), BF16),
                dma((CHUNKS, zp)), dma((CHUNKS, zp)), dma((CHUNKS, 3)), dma((CHUNKS, 3)),
                dma((CHUNKS,)), dma((CHUNKS,)),
                vmem((tokens, wgu.shape[2]), F32), vmem((tokens, wgu.shape[2] // 2), BF16),
                vmem((tokens, 128), F32),
            ],
            compiler_params=pltpu.CompilerParams(
                collective_id=0, has_side_effects=True, vmem_limit_bytes=60 * 1024 * 1024
            ),
        )(lens, hidden, queries, kv_cache, new_kv, gain.reshape(1, d_model), ids, rw, wo, wgu, wd)

    tok = P(("groups", "dev"), None)
    in_specs = (
        tok, tok, P(("groups", "dev"), None, None), tok, P(("groups", "dev")), P("dev", None),
        P(), tok, tok, P("dev", None, None), P("dev", None, None),
    )
    return jax.shard_map(step, mesh=mesh, in_specs=in_specs, out_specs=tok, check_vma=False)
```

time: 212 us -> 59.5 us (0.28)
  waiting for transfers between devices: 115 us -> 0 us
  Pallas kernels: 0 us -> 57.9 us
  blocking collectives: 37.8 us -> 0 us
  matrix products: 15.7 us -> 0 us
  between operations: 13.5 us -> 0.01 us
  local copies, waits for them, and re-layouts: 12.9 us -> 1.39 us
  starting transfers between devices: 11 us -> 0 us
  other arithmetic: 5.83 us -> 0 us
    psum x1 -> x0, waiting for transfers between devices: 92.3 us -> none  [shards(): resid_all = lax.psum(partial_value, 'dev')]
    pallas_call x0 -> x1, Pallas kernels: none -> 57.9 us  [step(): pl.pallas_call(functools.partial(kernel, n), out_shape=jax.ShapeDtypeStru...]
    all_gather x1 -> x0, blocking collectives: 37.8 us -> none  [shards(): every_route = lax.all_gather(route_ids, 'dev', axis=0, tiled=True)]
    all_to_all x2 -> x0, waiting for transfers between devices: 22.3 us -> none  [the longest x1 14.9 us: send_back(): lax.all_to_all(expert_out, 'dev', split_axis=0, concat_axis=0, tiled=True)]
    dot_general x8 -> x0, matrix products: 15.7 us -> none  [the longest x1 4.21 us: expert_rows(): jnp.einsum('smx,xf->smf', gathered_rows, gate_up, preferred_element_type=...]
    all_to_all x2 -> x0, starting transfers between devices: 10.9 us -> none  [the longest x1 7.3 us: shards(): lax.all_to_all(attn, 'dev', split_axis=1, concat_axis=0, tiled=True)]
    unnamed x21 -> x1, local copies, waits for them, and re-layouts: 4.88 us -> 1.39 us
    slice x1 -> x0, local copies, waits for them, and re-layouts: 3.2 us -> none  [attend(): cache_keys = kv_cache[:, :, :kv_width].reshape(seq_count, ctx_len, KVH, HD)]
  transfers between devices with their start and end apart: 3 -> 0, of which waited for: 3 -> 0; matrix products, arithmetic and copies ran while one was open for 1% -> 0% of each run, Pallas kernels for 0% -> 0%
where the time goes in v1:
time: 59.5 us; the launch traced here: 59.3 us
  Pallas kernels  57.9 us (97%)
  local copies, waits for them, and re-layouts  1.39 us (2%)
    pallas_call x1, Pallas kernels, step(): pl.pallas_call(functools.partial(kernel, n), out_shape=jax.ShapeDtypeStru...  57.9 us
    unnamed x1, local copies, waits for them, and re-layouts  1.39 us

profile of v1, /device:TPU:0, one launch (start us, length us, event | category | flops | bytes accessed | tf_op | source)
XLA Modules:
  0.0 59.3 jit_solution(13538183612333355092)
XLA Ops:
  0.0 57.9 %shard_map.109 = bf16[4,4096]{1,0:T(4,128)(2,1)} custom-call(s32[4]{0:T(128)} %lens.1, bf16[4,4096]{1,0:T(4,128)(2,1)} %hid.1, bf16[4,8192]{1,0:T(4,128)(2,1)} %q_ref.1, bf16[4,256,1024]{2,1,0:T(8,128)(2,1)} %kv_hbm.1, bf16[4,1024]{1,0:T(4,128)(2,1)} %new_ref.1, f32[1,4096]{1,0:T(1,128)} %bitcast.1, s32[4,8]{1,0:T(4,128)} %ids_ref.1, f32[4,8]{1,0:T(4,128)} %rw_ref.1, ...), custom_call_target="tpu_custom_call" | custom-call | tf_op jit(solution)/shard_map/pallas_call | solution.py:381
  57.9 1.4 %copy.13 = bf16[4,4096]{1,0:T(4,128)(2,1)} copy(bf16[4,4096]{1,0:T(4,128)(2,1)} %shard_map.109) | data formatting | bytes 65536

commit v2 on v1

v2 whole, which is shorter than its diff:
```python
import functools

import jax
import jax.numpy as jnp
from jax import lax
from jax.experimental import pallas as pl
from jax.experimental.pallas import tpu as pltpu
from jax.sharding import PartitionSpec as P

HEADS = 64
KVH = 4
HD = 128
TOPK = 8
PLANE = 8
CHUNKS = 4
SUB = 4
F32 = jnp.float32
BF16 = jnp.bfloat16


def dev_copy(src, dst, send, recv, target):
    return pltpu.make_async_remote_copy(
        src_ref=src, dst_ref=dst, send_sem=send, recv_sem=recv,
        device_id={"dev": target}, device_id_type=pl.DeviceIdType.MESH,
    )


def pick_matrix(tokens, cols, block, offset, z_count):
    row = lax.broadcasted_iota(jnp.int32, (tokens, cols), 0)
    col = lax.broadcasted_iota(jnp.int32, (tokens, cols), 1)
    zr = z_count * 4
    b = row & 3
    z = (row >> 2) & (z_count - 1)
    rest = row // zr
    second = rest & 1
    first = (rest >> 1) & 1
    core = rest >> 2
    x = jnp.where(core == 0, first, second)
    y = jnp.where(core == 0, second, first)
    src = z * 8 + y * 4 + x * 2 + core
    return jnp.where(col == src * block + offset + b, 1.0, 0.0).astype(BF16)


def kernel(
    n, lens, hid_hbm, q_hbm, kv_hbm, new_hbm, gain_hbm, ids_hbm, rw_hbm, wo_hbm, wgu_hbm, wd_hbm,
    out_ref,
    hid, q_ref, new_ref, gain_ref, ids_ref, rw_ref, kv, wo, wgu, wd, load_sem,
    asend, arecv, a_ss, a_rs,
    cz, cg, cz_ss, cz_rs, cg_ss, cg_rs,
    yb, yf, crx, qf, qb, p1rx, q2f, q2b, p2rx, zb, zf, zrx, res,
    rs_ss, rs_rs, z_ss, z_rs,
    nz, gx, nz_ss, nz_rs, ag_ss, ag_rs,
    gu, act, coef,
):
    me = lax.axis_index("dev")
    zc = n // PLANE
    zr = zc * 4
    tokens = 4 * n
    half = tokens // 2
    my_z = lax.div(me, PLANE)
    my_p = lax.rem(me, PLANE)
    my_y = lax.div(my_p, 4)
    my_x = lax.rem(lax.div(my_p, 2), 2)
    my_core = lax.rem(my_p, 2)
    first = (1 - my_core) * my_x + my_core * my_y
    second = (1 - my_core) * my_y + my_core * my_x
    step_x = (1 - 2 * my_x) * 2
    step_y = (1 - 2 * my_y) * 4
    peer1 = me + (1 - my_core) * step_x + my_core * step_y
    peer2 = me + (1 - my_core) * step_y + my_core * step_x
    mate = me + 1 - 2 * my_core
    d_model = out_ref.shape[1]
    cw = d_model // CHUNKS
    sw = cw // SUB
    ctx = kv.shape[1]
    kvw = KVH * HD
    per_group = HEADS // KVH
    hpd = HEADS // n
    dpg = n // KVH
    block = asend.shape[1]

    def z_at(j):
        return lax.rem(my_z + j, zc)

    def z_peer(j):
        return z_at(j) * PLANE + my_p

    barrier = pltpu.get_barrier_semaphore()

    @pl.loop(1, n)
    def _(k):
        pl.semaphore_signal(
            barrier, inc=1, device_id={"dev": lax.rem(me + k, n)},
            device_id_type=pl.DeviceIdType.MESH,
        )

    small = [
        pltpu.make_async_copy(src, dst, load_sem.at[i])
        for i, (src, dst) in enumerate(
            [
                (q_hbm, q_ref), (new_hbm, new_ref), (ids_hbm, ids_ref), (rw_hbm, rw_ref),
                (kv_hbm, kv), (hid_hbm, hid), (gain_hbm, gain_ref),
            ]
        )
    ]
    loads = [
        pltpu.make_async_copy(wo_hbm, wo, load_sem.at[7]),
        pltpu.make_async_copy(wgu_hbm.at[0], wgu, load_sem.at[8]),
        pltpu.make_async_copy(wd_hbm.at[0], wd, load_sem.at[9]),
    ]
    for load in small + loads:
        load.start()
    for load in small[:4]:
        load.wait()

    lane = lax.broadcasted_iota(jnp.int32, (4, 128), 1)
    ids = ids_ref[...]
    rw = rw_ref[...]
    own_coef = jnp.zeros((4, 128), F32)
    for k in range(TOPK):
        own_coef = own_coef + jnp.where(ids[:, k:k + 1] == (lane & 63), rw[:, k:k + 1], 0.0)
    high = own_coef.astype(BF16).astype(F32)
    packed = jnp.where(lane < 64, high, own_coef - high)
    cz[my_z] = jnp.concatenate([packed] * 4, axis=0).astype(BF16)

    rows = per_group * 4
    row_b = lax.broadcasted_iota(jnp.int32, (rows, 1), 0) & 3
    length = jnp.full((rows, 1), lens[0], jnp.int32)
    for b in range(1, 4):
        length = jnp.where(row_b == b, lens[b], length)
    live = lax.broadcasted_iota(jnp.int32, (rows, ctx), 1) < length
    new = new_ref[...].astype(F32)
    for load in small[4:]:
        load.wait()
    for g in range(KVH):
        q_all = q_ref[:, g * per_group * HD:(g + 1) * per_group * HD].astype(F32)
        qg = jnp.concatenate([q_all[:, r * HD:(r + 1) * HD] for r in range(per_group)], axis=0)
        k_own = jnp.concatenate([new[:, g * HD:(g + 1) * HD]] * per_group, axis=0)
        v_own = jnp.concatenate([new[:, kvw + g * HD:kvw + (g + 1) * HD]] * per_group, axis=0)
        q16 = qg.astype(BF16)
        scores = None
        for b in range(4):
            s_b = lax.dot_general(
                q16, kv[b, :, g * HD:(g + 1) * HD], (((1,), (1,)), ((), ())),
                preferred_element_type=F32,
            )
            scores = s_b if b == 0 else jnp.where(row_b == b, s_b, scores)
        scale = HD ** (-0.5)
        scores = jnp.where(live, scores * scale, -jnp.inf)
        fresh = jnp.sum(qg * k_own, axis=1, keepdims=True) * scale
        peak = jnp.maximum(jnp.max(scores, axis=1, keepdims=True), fresh)
        e = jnp.exp(scores - peak)
        e_own = jnp.exp(fresh - peak)
        den = jnp.sum(e, axis=1, keepdims=True) + e_own
        probs = e / den
        p_own = (e_own / den).astype(BF16).astype(F32)
        acc = p_own * v_own
        for b in range(4):
            p_b = jnp.where(row_b == b, probs, 0.0).astype(BF16)
            acc = acc + jnp.dot(
                p_b, kv[b, :, kvw + g * HD:kvw + (g + 1) * HD], preferred_element_type=F32
            )
        for i in range(dpg):
            piece = acc[i * hpd * 4:(i + 1) * hpd * 4, :]
            if piece.shape[0] < block:
                piece = jnp.concatenate([piece] * (block // piece.shape[0]), axis=0)
            asend[g * dpg + i] = piece.astype(BF16)

    pl.semaphore_wait(barrier, n - 1)

    @pl.loop(1, n)
    def _(k):
        target = lax.rem(me + k, n)
        dev_copy(asend.at[target], arecv.at[me], a_ss.at[target], a_rs.at[me], target).start()

    coef_out = []
    for j in range(1, zc):
        copy = dev_copy(
            cz.at[my_z], cz.at[my_z], cz_ss.at[j - 1], cz_rs.at[j - 1], z_peer(j)
        )
        copy.start()
        coef_out.append(copy)

    arecv[me] = asend[me]

    @pl.loop(1, n)
    def _(k):
        source = lax.rem(me + k, n)
        dev_copy(
            asend.at[source], arecv.at[source], a_ss.at[source], a_rs.at[source], source
        ).wait()

    x_all = arecv[...].astype(F32).reshape(n * block, HD).astype(BF16)
    gathered = jnp.concatenate(
        [
            jnp.dot(
                pick_matrix(tokens, n * block, block, rr * 4, zc), x_all,
                preferred_element_type=F32,
            )
            for rr in range(hpd)
        ],
        axis=1,
    ).astype(BF16)

    def reduce_chunks(t, make, done):
        ks = range(CHUNKS)
        cores = [
            dev_copy(
                yb.at[t, k, 1 - my_core], crx.at[t, k], rs_ss.at[t, k, 0], rs_rs.at[t, k, 0], mate
            )
            for k in ks
        ]
        firsts = [
            dev_copy(
                qb.at[t, k, 1 - first], p1rx.at[t, k], rs_ss.at[t, k, 1], rs_rs.at[t, k, 1], peer1
            )
            for k in ks
        ]
        seconds = [
            dev_copy(
                q2b.at[t, k, 1 - second], p2rx.at[t, k], rs_ss.at[t, k, 2], rs_rs.at[t, k, 2], peer2
            )
            for k in ks
        ]
        lines = [
            [
                dev_copy(
                    zb.at[t, k, z_at(j)], zrx.at[t, k, j - 1],
                    z_ss.at[t, k, j - 1], z_rs.at[t, k, j - 1], z_peer(j),
                )
                for j in range(1, zc)
            ]
            for k in range(CHUNKS)
        ]
        for k in range(CHUNKS):
            y = make(k).reshape(2, 2, 2, zr, cw)
            yb[t, k] = y.astype(BF16)
            cores[k].start()
            yf[k] = y
        for k in range(CHUNKS):
            cores[k].wait_recv()
            total = yf[k, my_core] + crx[t, k].astype(F32)
            qb[t, k] = total.astype(BF16)
            firsts[k].start()
            qf[k] = total
        for k in range(CHUNKS):
            firsts[k].wait_recv()
            total = qf[k, first] + p1rx[t, k].astype(F32)
            q2b[t, k] = total.astype(BF16)
            seconds[k].start()
            q2f[k] = total
        for k in range(CHUNKS):
            seconds[k].wait_recv()
            total = q2f[k, second] + p2rx[t, k].astype(F32)
            for z in range(zc):
                part = jnp.concatenate(
                    [total[4 * z:4 * z + 4, s * sw:(s + 1) * sw] for s in range(SUB)], axis=0
                )
                zb[t, k, z] = part.astype(BF16)
                zf[k, z] = part
            for copy in lines[k]:
                copy.start()
        for k in range(CHUNKS):
            total = zf[k, my_z]
            for j in range(1, zc):
                lines[k][j - 1].wait_recv()
                total = total + zrx[t, k, j - 1].astype(F32)
            done(k, total)
        for k in range(CHUNKS):
            for copy in [cores[k], firsts[k], seconds[k]] + lines[k]:
                copy.wait_send()

    for j in range(1, zc):
        from_z = z_at(zc - j)
        dev_copy(
            cz.at[from_z], cz.at[from_z], cz_ss.at[j - 1], cz_rs.at[j - 1], z_peer(j)
        ).wait_recv()
    cg[my_core, first, second] = jnp.concatenate(
        [cz[z].astype(F32)[0:4, :] for z in range(zc)], axis=0
    ).astype(BF16)

    def spread(ref, stage, send, recv):
        here, there, target = [
            (ref.at[my_core, first, second], ref.at[my_core, first, 1 - second], peer2),
            (ref.at[my_core, first], ref.at[my_core, 1 - first], peer1),
            (ref.at[my_core], ref.at[1 - my_core], mate),
        ][stage]
        out = dev_copy(here, here, send, recv, target)
        arrive = dev_copy(there, there, send, recv, target)
        return out, arrive

    coef_steps = [spread(cg, i, cg_ss.at[i], cg_rs.at[i]) for i in range(3)]
    coef_steps[0][0].start()

    loads[0].wait()

    def project(k):
        return jnp.dot(gathered, wo[:, k * cw:(k + 1) * cw], preferred_element_type=F32)

    hidden = hid[...].astype(F32)
    squares = []

    def add_hidden(k, total):
        own = jnp.concatenate(
            [hidden[:, k * cw + s * sw:k * cw + (s + 1) * sw] for s in range(SUB)], axis=0
        )
        value = total + own
        res[k] = value
        squares.append(jnp.sum(value * value, axis=1, keepdims=True))

    reduce_chunks(0, project, add_hidden)

    coef_steps[0][1].wait_recv()
    coef_steps[1][0].start()
    square = sum(squares[1:], squares[0])
    square = square[0:4] + square[4:8] + square[8:12] + square[12:16]
    inverse = lax.rsqrt(square / d_model + 1e-06)
    inverse = jnp.concatenate([inverse] * SUB, axis=0)

    line_out = []
    for k in range(CHUNKS):
        gain = jnp.concatenate(
            [
                jnp.broadcast_to(
                    gain_ref[:, k * cw + s * sw:k * cw + (s + 1) * sw], (4, sw)
                )
                for s in range(SUB)
            ],
            axis=0,
        )
        nz[k, my_z] = (res[k] * inverse * gain).astype(BF16)
        for j in range(1, zc):
            copy = dev_copy(
                nz.at[k, my_z], nz.at[k, my_z], nz_ss.at[k, j - 1], nz_rs.at[k, j - 1], z_peer(j)
            )
            copy.start()
            line_out.append(copy)
    steps = [
        [spread(gx.at[k], i, ag_ss.at[k, i], ag_rs.at[k, i]) for i in range(3)]
        for k in range(CHUNKS)
    ]
    for k in range(CHUNKS):
        for j in range(1, zc):
            from_z = z_at(zc - j)
            dev_copy(
                nz.at[k, from_z], nz.at[k, from_z], nz_ss.at[k, j - 1], nz_rs.at[k, j - 1], z_peer(j)
            ).wait_recv()
        parts = []
        for z in range(zc):
            value = nz[k, z].astype(F32)
            parts.append(
                jnp.concatenate([value[4 * s:4 * s + 4, :] for s in range(SUB)], axis=1)
            )
        gx[k, my_core, first, second] = jnp.concatenate(parts, axis=0).astype(BF16)
        steps[k][0][0].start()
    coef_steps[1][1].wait_recv()
    coef_steps[2][0].start()
    for stage in (1, 2):
        for k in range(CHUNKS):
            steps[k][stage - 1][1].wait_recv()
            steps[k][stage][0].start()

    coef_steps[2][1].wait_recv()
    lane_t = lax.broadcasted_iota(jnp.int32, (tokens, 128), 1) & 63
    all_coef = cg[...].reshape(tokens, 128).astype(F32)
    coef[...] = jnp.broadcast_to(
        jnp.sum(
            jnp.where(lane_t == lax.div(me, 2), all_coef, 0.0), axis=1, keepdims=True
        ),
        (tokens, 128),
    )

    loads[1].wait()
    for k in range(CHUNKS):
        steps[k][2][1].wait_recv()
        part = jnp.dot(
            gx[k].reshape(tokens, cw), wgu[k * cw:(k + 1) * cw, :], preferred_element_type=F32
        )
        if k == 0:
            gu[...] = part
        else:
            gu[...] += part
    for copy in line_out + coef_out:
        copy.wait_send()
    for group in steps + [coef_steps]:
        for out, _ in group:
            out.wait_send()
    ff = gu.shape[1] // 2
    gate = gu[:, :ff]
    act[...] = (gate / (1.0 + jnp.exp(-gate)) * gu[:, ff:]).astype(BF16)

    loads[2].wait()

    def expert_out(k):
        y = jnp.dot(act[...], wd[:, k * cw:(k + 1) * cw], preferred_element_type=F32)
        return y.astype(BF16).astype(F32) * coef[:, 0:1]

    def finish(k, total):
        value = (res[k] + total).astype(out_ref.dtype).astype(F32)
        for s in range(SUB):
            lo = k * cw + s * sw
            out_ref[:, lo:lo + sw] = value[4 * s:4 * s + 4, :].astype(out_ref.dtype)

    reduce_chunks(1, expert_out, finish)


def solution(mesh):
    n = mesh.shape["dev"]

    def step(hidden, queries, kv_cache, new_kv, lens, wo, gain, ids, rw, wgu, wd):
        seqs, d_model = hidden.shape
        zc = n // PLANE
        zr = zc * 4
        tokens = n * seqs
        cw = d_model // CHUNKS
        sw = cw // SUB
        block = max(8, HEADS // n * 4)
        dma = pltpu.SemaphoreType.DMA
        vmem = pltpu.VMEM
        any_spec = pl.BlockSpec(memory_space=pl.ANY)
        v_spec = pl.BlockSpec(memory_space=pltpu.VMEM)
        zp = max(1, zc - 1)
        return pl.pallas_call(
            functools.partial(kernel, n),
            out_shape=jax.ShapeDtypeStruct((seqs, d_model), BF16),
            in_specs=[pl.BlockSpec(memory_space=pltpu.SMEM)] + [any_spec] * 10,
            out_specs=v_spec,
            scratch_shapes=[
                vmem(hidden.shape, BF16), vmem(queries.shape, BF16), vmem(new_kv.shape, BF16),
                vmem((1, d_model), F32), vmem(ids.shape, jnp.int32), vmem(rw.shape, F32),
                vmem(kv_cache.shape, BF16), vmem(wo.shape, BF16), vmem(wgu.shape[1:], BF16),
                vmem(wd.shape[1:], BF16), dma((10,)),
                vmem((n, block, HD), BF16), vmem((n, block, HD), BF16), dma((n,)), dma((n,)),
                vmem((zc, 16, 128), BF16), vmem((2, 2, 2, zr, 128), BF16),
                dma((zp,)), dma((zp,)), dma((3,)), dma((3,)),
                vmem((2, CHUNKS, 2, 2, 2, zr, cw), BF16), vmem((CHUNKS, 2, 2, 2, zr, cw), F32),
                vmem((2, CHUNKS, 2, 2, zr, cw), BF16), vmem((CHUNKS, 2, 2, zr, cw), F32),
                vmem((2, CHUNKS, 2, 2, zr, cw), BF16), vmem((2, CHUNKS, 2, zr, cw), BF16),
                vmem((CHUNKS, 2, zr, cw), F32), vmem((2, CHUNKS, 2, zr, cw), BF16),
                vmem((2, CHUNKS, zr, cw), BF16),
                vmem((2, CHUNKS, zc, 4 * SUB, sw), BF16), vmem((CHUNKS, zc, 4 * SUB, sw), F32),
                vmem((2, CHUNKS, zp, 4 * SUB, sw), BF16), vmem((CHUNKS, 4 * SUB, sw), F32),
                dma((2, CHUNKS, 3)), dma((2, CHUNKS, 3)), dma((2, CHUNKS, zp)), dma((2, CHUNKS, zp)),
                vmem((CHUNKS, zc, 4 * SUB, sw), BF16), vmem((CHUNKS, 2, 2, 2, zr, cw), BF16),
                dma((CHUNKS, zp)), dma((CHUNKS, zp)), dma((CHUNKS, 3)), dma((CHUNKS, 3)),
                vmem((tokens, wgu.shape[2]), F32), vmem((tokens, wgu.shape[2] // 2), BF16),
                vmem((tokens, 128), F32),
            ],
            compiler_params=pltpu.CompilerParams(
                collective_id=0, has_side_effects=True, vmem_limit_bytes=60 * 1024 * 1024
            ),
        )(lens, hidden, queries, kv_cache, new_kv, gain.reshape(1, d_model), ids, rw, wo, wgu, wd)

    tok = P(("groups", "dev"), None)
    in_specs = (
        tok, tok, P(("groups", "dev"), None, None), tok, P(("groups", "dev")), P("dev", None),
        P(), tok, tok, P("dev", None, None), P("dev", None, None),
    )
    return jax.shard_map(step, mesh=mesh, in_specs=in_specs, out_specs=tok, check_vma=False)
```

time: 59.5 us -> 60.5 us (1.017)
  Pallas kernels: 57.9 us -> 58.9 us
    pallas_call x1, Pallas kernels: 57.9 us -> 58.9 us  [step(): pl.pallas_call(functools.partial(kernel, n), out_shape=jax.ShapeDtypeStru...]
where the time goes in v2:
time: 60.5 us; the launch traced here: 60.3 us
  Pallas kernels  58.9 us (97%)
  local copies, waits for them, and re-layouts  1.39 us (2%)
    pallas_call x1, Pallas kernels, step(): pl.pallas_call(functools.partial(kernel, n), out_shape=jax.ShapeDtypeStru...  58.9 us
    unnamed x1, local copies, waits for them, and re-layouts  1.39 us

profile of v2, /device:TPU:0, one launch (start us, length us, event | category | flops | bytes accessed | tf_op | source)
XLA Modules:
  0.0 60.3 jit_solution(9102326402312728504)
XLA Ops:
  0.0 58.9 %shard_map.109 = bf16[4,4096]{1,0:T(4,128)(2,1)} custom-call(s32[4]{0:T(128)} %lens.1, bf16[4,4096]{1,0:T(4,128)(2,1)} %hid_hbm.1, bf16[4,8192]{1,0:T(4,128)(2,1)} %q_hbm.1, bf16[4,256,1024]{2,1,0:T(8,128)(2,1)} %kv_hbm.1, bf16[4,1024]{1,0:T(4,128)(2,1)} %new_hbm.1, f32[1,4096]{1,0:T(1,128)} %bitcast.1, s32[4,8]{1,0:T(4,128)} %ids_hbm.1, f32[4,8]{1,0:T(4,128)} %rw_hbm.1, ...), custom_call_target="tpu_custom_call" | custom-call | tf_op jit(solution)/shard_map/pallas_call | solution.py:423
  58.9 1.4 %copy.13 = bf16[4,4096]{1,0:T(4,128)(2,1)} copy(bf16[4,4096]{1,0:T(4,128)(2,1)} %shard_map.109) | data formatting | bytes 65536

commit v3 on v2

--- a/solution.py
+++ b/solution.py
@@ -335,11 +335,30 @@
             )
             copy.start()
             line_out.append(copy)
-    steps = [
-        [spread(gx.at[k], i, ag_ss.at[k, i], ag_rs.at[k, i]) for i in range(3)]
-        for k in range(CHUNKS)
-    ]
-    for k in range(CHUNKS):
+    diagonal = peer1 + peer2 - me
+
+    def plane_copies(k):
+        here = gx.at[k, my_core, first, second]
+        copies = []
+        for i, (f, h, target) in enumerate(
+            [
+                (1 - first, 1 - second, diagonal), (1 - first, second, peer1),
+                (first, 1 - second, peer2),
+            ]
+        ):
+            there = gx.at[k, my_core, f, h]
+            copies.append(
+                (
+                    dev_copy(here, here, ag_ss.at[k, i], ag_rs.at[k, i], target),
+                    dev_copy(there, there, ag_ss.at[k, i], ag_rs.at[k, i], target),
+                )
+            )
+        return copies
+
+    planes = [plane_copies(k) for k in range(CHUNKS)]
+    mates = [spread(gx.at[k], 2, ag_ss.at[k, 3], ag_rs.at[k, 3]) for k in range(CHUNKS)]
+
+    def gather_plane(k):
         for j in range(1, zc):
             from_z = z_at(zc - j)
             dev_copy(
@@ -352,13 +371,32 @@
                 jnp.concatenate([value[4 * s:4 * s + 4, :] for s in range(SUB)], axis=1)
             )
         gx[k, my_core, first, second] = jnp.concatenate(parts, axis=0).astype(BF16)
-        steps[k][0][0].start()
-    coef_steps[1][1].wait_recv()
-    coef_steps[2][0].start()
-    for stage in (1, 2):
-        for k in range(CHUNKS):
-            steps[k][stage - 1][1].wait_recv()
-            steps[k][stage][0].start()
+        for out, _ in planes[k]:
+            out.start()
+
+    def gather_mate(k):
+        for _, arrive in planes[k]:
+            arrive.wait_recv()
+        mates[k][0].start()
+
+    def gate_up(k):
+        mates[k][1].wait_recv()
+        part = jnp.dot(
+            gx[k].reshape(tokens, cw), wgu[k * cw:(k + 1) * cw, :], preferred_element_type=F32
+        )
+        if k == 0:
+            gu[...] = part
+        else:
+            gu[...] += part
+
+    gathers = [gather_plane, gather_mate, gate_up]
+    for at, stage in enumerate(gathers):
+        if at == 2:
+            loads[1].wait()
+            coef_steps[1][1].wait_recv()
+            coef_steps[2][0].start()
+        for k in range(CHUNKS):
+            stage(k)
 
     coef_steps[2][1].wait_recv()
     lane_t = lax.broadcasted_iota(jnp.int32, (tokens, 128), 1) & 63
@@ -370,19 +408,9 @@
         (tokens, 128),
     )
 
-    loads[1].wait()
-    for k in range(CHUNKS):
-        steps[k][2][1].wait_recv()
-        part = jnp.dot(
-            gx[k].reshape(tokens, cw), wgu[k * cw:(k + 1) * cw, :], preferred_element_type=F32
-        )
-        if k == 0:
-            gu[...] = part
-        else:
-            gu[...] += part
     for copy in line_out + coef_out:
         copy.wait_send()
-    for group in steps + [coef_steps]:
+    for group in planes + [mates, coef_steps]:
         for out, _ in group:
             out.wait_send()
     ff = gu.shape[1] // 2
@@ -442,7 +470,7 @@
                 vmem((2, CHUNKS, zp, 4 * SUB, sw), BF16), vmem((CHUNKS, 4 * SUB, sw), F32),
                 dma((2, CHUNKS, 3)), dma((2, CHUNKS, 3)), dma((2, CHUNKS, zp)), dma((2, CHUNKS, zp)),
                 vmem((CHUNKS, zc, 4 * SUB, sw), BF16), vmem((CHUNKS, 2, 2, 2, zr, cw), BF16),
-                dma((CHUNKS, zp)), dma((CHUNKS, zp)), dma((CHUNKS, 3)), dma((CHUNKS, 3)),
+                dma((CHUNKS, zp)), dma((CHUNKS, zp)), dma((CHUNKS, 4)), dma((CHUNKS, 4)),
                 vmem((tokens, wgu.shape[2]), F32), vmem((tokens, wgu.shape[2] // 2), BF16),
                 vmem((tokens, 128), F32),
             ],

time: 60.5 us -> 56.5 us (0.934)
  Pallas kernels: 58.9 us -> 55 us
    pallas_call x1, Pallas kernels: 58.9 us -> 55 us  [step(): pl.pallas_call(functools.partial(kernel, n), out_shape=jax.ShapeDtypeStru...]
where the time goes in v3:
time: 56.5 us; the launch traced here: 56.4 us
  Pallas kernels  55 us (97%)
  local copies, waits for them, and re-layouts  1.39 us (2%)
    pallas_call x1, Pallas kernels, step(): pl.pallas_call(functools.partial(kernel, n), out_shape=jax.ShapeDtypeStru...  55 us
    unnamed x1, local copies, waits for them, and re-layouts  1.39 us

profile of v3, /device:TPU:0, one launch (start us, length us, event | category | flops | bytes accessed | tf_op | source)
XLA Modules:
  0.0 56.4 jit_solution(5039048657802433822)
XLA Ops:
  0.0 55.0 %shard_map.109 = bf16[4,4096]{1,0:T(4,128)(2,1)} custom-call(s32[4]{0:T(128)} %lens.1, bf16[4,4096]{1,0:T(4,128)(2,1)} %hid_hbm.1, bf16[4,8192]{1,0:T(4,128)(2,1)} %q_hbm.1, bf16[4,256,1024]{2,1,0:T(8,128)(2,1)} %kv_hbm.1, bf16[4,1024]{1,0:T(4,128)(2,1)} %new_hbm.1, f32[1,4096]{1,0:T(1,128)} %bitcast.1, s32[4,8]{1,0:T(4,128)} %ids_hbm.1, f32[4,8]{1,0:T(4,128)} %rw_hbm.1, ...), custom_call_target="tpu_custom_call" | custom-call | tf_op jit(solution)/shard_map/pallas_call | solution.py:451
  55.0 1.4 %copy.13 = bf16[4,4096]{1,0:T(4,128)(2,1)} copy(bf16[4,4096]{1,0:T(4,128)(2,1)} %shard_map.109) | data formatting | bytes 65536
